TPU v7x, 32 devices: a whole 2x2x4 slice. The times are simulated.
32 devices in a mesh: section: 4 (over y, core), dp: 8 (over z, x).
Axes of the slice: x: 2, y: 2, z: 4, core: 2. Of those that a mesh axis runs over, the one named last changes fastest.
Arguments:
- activations: bfloat16 [4, 2048, 8192], P('section', 'dp'), may hold values from -600 to 600, as said below
- tail_grads: bfloat16 [4, 2048, 512], P('section', 'dp'), may hold values from -48 to 48, as said below
- tail_slots: int32 [4, 8, 4], P('section', 'dp'), may hold values from 0 to 3, each once within a row
- master: float32 [4, 8192, 512], P('section', 'dp'), may hold values from -6 to 6
- moment1: float32 [4, 8192, 512], P('section', 'dp'), may hold values from -0.00029296876 to 0.00029296876
- moment2: float32 [4, 8192, 512], P('section', 'dp'), may hold values from 1.1920929e-09 to 2.9802322e-08
- overflow: int32 [4, 8], P('section', 'dp'), may hold values from 0 to 1, as said below
- clip_on: int32 [4], P('section'), may hold values from 0 to 1, as said below
- next_inputs: bfloat16 [4, 256, 8192], P('section', 'dp'), may hold values from -6 to 6
Outputs:
- new_master: float32 [4, 8192, 512], P('section', 'dp')
- next_out: bfloat16 [4, 256, 512], P('section', 'dp')
Inputs may be any that keep to these rules, and one draw needn't show every extreme that they name: `tail_slots`: each row along the last dimension names every slot once. `overflow`: at least one shard is flagged and at least one is not. `clip_on`: at least one section is clipped and at least one is not. `activations`: real-valued. `tail_grads`: real-valued.
All inputs are finite; a program needn't handle non-finite values.
Results may differ from a plain program's by a relative error of at most 0.0049.
Values may be sent and summed in bfloat16 or wider, within the bound.
A program may use at most 64 MiB of HBM per device.

v0:
```python
import math

import jax
import jax.numpy as jnp
from jax import lax
from jax.sharding import PartitionSpec as P

beta_one = 0.9
beta_two = 0.95
correct_one = 1.0 - 0.9**20
correct_two = 1.0 - 0.95**20
adam_eps = 1e-08
decay_rate = 0.1
learn_rate = 0.1


def local(
    activations, tail_grads, tail_slots, master, moment1, moment2, overflow, clip_on, next_inputs
):
    stashed = activations[0]
    local_tails = tail_grads[0]
    slots = tail_slots[0, 0]
    tail_count = slots.shape[0]
    tok_dev, width = stashed.shape
    slab_cols = local_tails.shape[1]
    dp_count = lax.axis_size("dp")
    onehot = (slots[:, None] == jnp.arange(tail_count, dtype=jnp.int32)[None, :]).astype(
        jnp.float32
    )
    shaped = local_tails.reshape(tail_count, tok_dev // tail_count, slab_cols).astype(jnp.float32)
    paired = (
        jnp.einsum("tk,tnc->knc", onehot, shaped).astype(jnp.bfloat16).reshape(tok_dev, slab_cols)
    )
    contract = (((0,), (0,)), ((), ()))
    feature_block = lax.all_to_all(stashed, "dp", split_axis=1, concat_axis=0, tiled=True)
    block = feature_block
    summed = lax.dot_general(
        block,
        lax.all_gather(paired, "dp", axis=0, tiled=True),
        contract,
        preferred_element_type=jnp.float32,
    )
    gradient = summed * (1.0 / (tok_dev * dp_count))
    keep = (overflow[0, 0] == 0).astype(jnp.float32)
    partial_sq = keep * jnp.sum(gradient * gradient)
    sumsq = lax.psum(partial_sq, ("section", "dp"))
    norm_value = jnp.sqrt(sumsq)
    factor = jnp.where(clip_on[0] == 1, 1.0 / jnp.maximum(norm_value, 1.0), 1.0)
    clipped = gradient * factor
    old_master = master[0]
    m_next = beta_one * moment1[0] + (1.0 - beta_one) * clipped
    v_next = beta_two * moment2[0] + (1.0 - beta_two) * (clipped * clipped)
    update = (
        m_next / correct_one / (jnp.sqrt(v_next / correct_two) + adam_eps) + decay_rate * old_master
    )
    updated = jnp.where(keep > 0.5, old_master - learn_rate * update, old_master)
    weights = updated.astype(jnp.bfloat16)
    inputs = next_inputs[0]
    block = inputs
    result = jnp.dot(
        block, lax.all_gather(weights, "dp", axis=0, tiled=True), preferred_element_type=jnp.float32
    )
    next_out = (result * (1.0 / math.sqrt(width))).astype(jnp.bfloat16)
    return (updated[None], next_out[None])


def solution(mesh):
    return jax.shard_map(
        local,
        mesh=mesh,
        in_specs=(
            P("section", "dp", None),
            P("section", "dp", None),
            P("section", "dp", None),
            P("section", "dp", None),
            P("section", "dp", None),
            P("section", "dp", None),
            P("section", "dp"),
            P("section"),
            P("section", "dp", None),
        ),
        out_specs=(P("section", "dp", None), P("section", "dp", None)),
        check_vma=False,
    )
```

profile of v0, /device:TPU:0, one launch (start us, length us, event | category | flops | bytes accessed | tf_op | source)
XLA Modules:
  0.0 338.0 jit_solution(18215369352507247431)
XLA Ops:
  7.2 0.0 copy-start
  7.2 6.5 %copy.26 = bf16[1,256,8192]{1,2,0:T(8,128)(2,1)} copy(bf16[1,256,8192]{2,1,0:T(8,128)(2,1)} %param.9) | data formatting | bytes 8388608 | tf_op args[0]
  13.7 0.0 copy-start.1
  13.7 0.0 copy-start.2
  13.7 7.4 %all-to-all-start = ((bf16[256,8,1024]{0,2,1:T(8,128)(2,1)}), bf16[256,8,1024]{0,2,1:T(8,128)(2,1)}, u32[]{:S(2)}, u32[]{:S(2)}) async-start(bf16[256,8,1024]{0,2,1:T(8,128)(2,1)} %bitcast.58), calls=%async_computation | async-start | bytes 8388608 | tf_op jit(solution)/shard_map/all_to_all | solution.py:35
  21.1 0.0 all-gather.3.cloned.1.call-start
  21.1 0.0 copy-done.1
  21.1 0.0 copy-done.2
  21.1 0.3 convolution_convert_fusion
  21.4 0.8 copy.25
  22.2 0.0 all-gather.3.cloned.1.call-update
  22.2 0.0 all-gather.5.cloned.1.call-start
  23.5 1.9 copy.22
  25.5 2.9 copy.23
  28.4 2.9 copy.28
  31.3 108.3 %all-to-all-done = bf16[256,8,1024]{0,2,1:T(8,128)(2,1)} async-done(((bf16[256,8,1024]{0,2,1:T(8,128)(2,1)}), bf16[256,8,1024]{0,2,1:T(8,128)(2,1)}, u32[]{:S(2)}, u32[]{:S(2)}) %all-to-all-start) | async-done | bytes 4194336 | tf_op jit(solution)/shard_map/all_to_all | solution.py:35
  139.6 6.5 %copy.27 = bf16[8,256,1024]{2,1,0:T(8,128)(2,1)} copy(bf16[8,256,1024]{1,2,0:T(8,128)(2,1)} %bitcast.8) | data formatting | bytes 8388608 | tf_op jit(solution)/shard_map/all_to_all | solution.py:35
  146.1 0.0 all-gather.3.cloned.1.call-done
  146.1 7.1 %multiply_reduce_fusion = (f32[]{:T(128)}, f32[512,1024]{1,0:T(8,128)}) fusion(bf16[2048,512]{1,0:T(8,128)(2,1)} %all-gather.3.cloned.1.call-done, bf16[2048,1024]{1,0:T(8,128)(2,1)} %bitcast.60), kind=kOutput, calls=%fused_computation.11 | convolution fusion | flops 2149056512 | bytes 8388612 | tf_op jit(solution)/shard_map/dot_general | solution.py:37
  153.9 37.8 %psum.7 = f32[]{:T(128)} all-reduce(f32[]{:T(128)S(6)} %mul.79), channel_id=1, replica_groups=mesh['section'=4,'dp'=8] {'section','dp'}, use_global_device_ids=true, to_apply=%region_1.0 | all-reduce | flops 1 | bytes 8 | tf_op jit(solution)/shard_map/psum | solution.py:46
  192.4 6.3 %fusion.14 = (bf16[1024,512]{0,1:T(8,128)(2,1)}, f32[1024,512]{0,1:T(8,128)}) fusion(f32[1,1024,512]{1,2,0:T(8,128)} %copy.28, f32[512,1024]{1,0:T(8,128)} %get-tuple-element.11, f32[]{:T(128)S(6)} %mul.80, f32[1,1024,512]{1,2,0:T(8,128)} %copy.23, f32[1,1024,512]{1,2,0:T(8,128)S(1)} %copy.22, pred[]{:T(512)S(6)} %gt.3), kind=kLoop, calls=%fused_computation.21 | loop fusion | flops 9437184 | bytes 11534341 | tf_op jit(solution)/shard_map/convert_element_type | solution.py:57
  198.8 0.0 all-gather.5.cloned.1.call-update
  198.8 2.9 copy.29
  201.7 122.8 %all-gather.5.cloned.1.call-done = bf16[8192,512]{0,1:T(8,128)(2,1)} async-done(((bf16[1024,512]{0,1:T(8,128)(2,1)}), bf16[8192,512]{0,1:T(8,128)(2,1)}) %all-gather.5.cloned.1.call-update) | async-done | bytes 8388624 | tf_op jit(solution)/shard_map/all_gather | solution.py:61
  324.5 0.0 copy-done
  324.5 6.6 %fusion.8 = bf16[1,32,512]{2,1,0:T(8,128)(2,1)} fusion(bf16[8192,512]{0,1:T(8,128)(2,1)} %all-gather.5.cloned.1.call-done, bf16[1,32,8192]{2,1,0:T(8,128)(2,1)S(1)} %copy-done), kind=kOutput, calls=%fused_computation.15 | convolution fusion | flops 268468224 | bytes 8945664 | tf_op jit(solution)/shard_map/dot_general | solution.py:60
Async XLA Ops:
  7.2 317.4 %copy-start = (bf16[1,32,8192]{2,1,0:T(8,128)(2,1)S(1)}, bf16[1,32,8192]{2,1,0:T(8,128)(2,1)}, u32[]{:S(2)}) copy-start(bf16[1,32,8192]{2,1,0:T(8,128)(2,1)} %param.17) | copy-start | bytes 1572868
  13.7 7.4 %copy-start.1 = (bf16[1,256,512]{2,1,0:T(8,128)(2,1)S(1)}, bf16[1,256,512]{2,1,0:T(8,128)(2,1)}, u32[]{:S(2)}) copy-start(bf16[1,256,512]{2,1,0:T(8,128)(2,1)} %param.10) | copy-start | bytes 786436
  13.7 7.4 %copy-start.2 = (s32[1,1,4]{2,1,0:T(1,128)S(1)}, s32[1,1,4]{2,1,0:T(1,128)}, u32[]{:S(2)}) copy-start(s32[1,1,4]{2,1,0:T(1,128)} %param.11) | copy-start | bytes 52
  13.7 125.9 %all-to-all-start = ((bf16[256,8,1024]{0,2,1:T(8,128)(2,1)}), bf16[256,8,1024]{0,2,1:T(8,128)(2,1)}, u32[]{:S(2)}, u32[]{:S(2)}) async-start(bf16[256,8,1024]{0,2,1:T(8,128)(2,1)} %bitcast.58), calls=%async_computation | async-start | bytes 8388608 | tf_op jit(solution)/shard_map/all_to_all | solution.py:35
  21.1 125.0 %all-gather.3.cloned.1.call-start = ((), (), s32[]{:S(2)}) async-start(), calls=%async_computation.1 | async-start | bytes 2359296 | tf_op jit(solution)/shard_map/all_gather | solution.py:39
  22.2 302.3 %all-gather.5.cloned.1.call-start = ((), (), s32[]{:S(2)}) async-start(), calls=%async_computation.2 | async-start | bytes 9437184 | tf_op jit(solution)/shard_map/all_gather | solution.py:61
Sparse Core Ops, SparseCore 0:
  24.0 103.1 all-gather.2
  198.9 125.5 all-gather.4
where the time goes:
time: 339 us; the launch traced here: 338 us
  waiting for transfers between devices  231 us (68%)
  blocking collectives  37.8 us (11%)
  local copies, waits for them, and re-layouts  24.3 us (7%)
  between operations  16.8 us (5%)
  matrix products  14 us (4%)
  starting transfers between devices  7.46 us (2%)
  other arithmetic  6.34 us (2%)
    all_gather x1, waiting for transfers between devices, local(): lax.all_gather(weights, 'dp', axis=0, tiled=True)  123 us
    all_to_all x1, waiting for transfers between devices, local(): lax.all_to_all(stashed, 'dp', split_axis=1, concat_axis=0, tiled=True)  108 us
    psum x1, blocking collectives, local(): sumsq = lax.psum(partial_sq, ('section', 'dp'))  37.8 us
    unnamed x11, local copies, waits for them, and re-layouts  17.1 us
    all_to_all x1, starting transfers between devices, local(): lax.all_to_all(stashed, 'dp', split_axis=1, concat_axis=0, tiled=True)  7.38 us
    dot_general x1, matrix products, local(): lax.dot_general(block, lax.all_gather(paired, 'dp', axis=0, tiled=True),...  7.12 us
  transfers between devices with their start and end apart: 3, of which 2 were waited for; matrix products, arithmetic and copies ran while one was open for 5% of the time, Pallas kernels for 0%

commit v1 on v0

v1 whole, which is shorter than its diff:
```python
import functools
import math

import jax
import jax.numpy as jnp
from jax import lax
from jax.experimental import pallas as pl
from jax.experimental.pallas import tpu as pltpu
from jax.sharding import PartitionSpec as P

MESH = pl.DeviceIdType.MESH
beta_one = 0.9
beta_two = 0.95
correct_one = 1.0 - 0.9**20
correct_two = 1.0 - 0.95**20
adam_eps = 1e-08
decay_rate = 0.1
learn_rate = 0.1


def remote(src, dst, send, recv, where):
    return pltpu.make_async_remote_copy(
        src_ref=src, dst_ref=dst, send_sem=send, recv_sem=recv, device_id=where,
        device_id_type=MESH,
    )


def kernel(
    n, sections, step,
    act, tails, slots, master_in, m1_in, m2_in, overflow, clip_on, nxt,
    master_out, next_out,
    far, near, paired, master, m1, m2, grad, psend, precv, weights, inputs, part, landed,
    sq_dp, sq_sec, sq_mine, sq_sum,
    load_sem, far_s, far_r, near_s, near_r, pair_s, pair_r, p_s, p_r, in_s, in_r, out_s, out_r,
    sd_s, sd_r, ss_s, ss_r,
):
    tok, width = act.shape
    rows, cols = master.shape
    nrows = nxt.shape[0]
    tail_count = slots.shape[-1]
    tail_tok = tok // tail_count
    group = n // 2
    me = lax.axis_index("dp")
    sec = lax.axis_index("section")
    half = me // group
    low = lax.rem(me, group)
    other = 1 - half
    pieces = rows // step

    def each(count, body):
        lax.fori_loop(1, count, lambda j, c: (body(j), c)[1], 0)

    barrier = pltpu.get_barrier_semaphore()
    each(n, lambda j: pl.semaphore_signal(
        barrier, inc=1, device_id={"dp": lax.rem(me + j, n)}, device_id_type=MESH))
    each(sections, lambda j: pl.semaphore_signal(
        barrier, inc=1, device_id={"section": lax.rem(sec + j, sections)}, device_id_type=MESH))

    def feature(dev):
        return pl.ds(pl.multiple_of(dev * rows, rows), rows)

    def block(ref, index, size):
        return ref.at[pl.ds(pl.multiple_of(index * size, size), size)]

    loads = [
        pltpu.make_async_copy(
            act.at[:, feature(other * group + low)], block(far, low, tok), load_sem.at[0]),
        pltpu.make_async_copy(
            act.at[:, feature(me)], block(near, low, tok), load_sem.at[1]),
        pltpu.make_async_copy(
            nxt.at[:, feature(me)], block(inputs, me, nrows), load_sem.at[2]),
        pltpu.make_async_copy(master_in, master, load_sem.at[3]),
        pltpu.make_async_copy(m1_in, m1, load_sem.at[4]),
        pltpu.make_async_copy(m2_in, m2, load_sem.at[5]),
    ]
    for load in loads:
        load.start()

    mine = pl.multiple_of(low * tok, tok)
    for k in range(tail_count):
        value = tails[0:tail_tok, :]
        for t in range(1, tail_count):
            value = jnp.where(
                slots[0, t] == k, tails[t * tail_tok:(t + 1) * tail_tok, :], value)
        paired[pl.ds(mine + k * tail_tok, tail_tok), :] = value

    pl.semaphore_wait(barrier, n - 1 + sections - 1)

    def peer(j):
        return lax.rem(low + j, group)

    def pair_copy(to, slot):
        return remote(block(paired, low, tok), block(paired, slot, tok), pair_s.at[to],
                      pair_r.at[slot], {"dp": half * group + to})

    def far_copy(to, slot):
        return remote(act.at[:, feature(other * group + to)], block(far, slot, tok),
                      far_s.at[to], far_r.at[slot], {"dp": half * group + to})

    def near_copy(to, slot):
        return remote(act.at[:, feature(half * group + to)], block(near, slot, tok),
                      near_s.at[to], near_r.at[slot], {"dp": half * group + to})

    each(group, lambda j: pair_copy(peer(j), low).start())
    each(group, lambda j: far_copy(peer(j), low).start())
    each(group, lambda j: near_copy(peer(j), low).start())

    contract = (((0,), (0,)), ((), ()))

    loads[0].wait()
    each(group, lambda j: pair_copy(peer(j), peer(j)).wait_recv())
    each(group, lambda j: far_copy(peer(j), peer(j)).wait_recv())

    def part_copy(c):
        return remote(psend.at[c], precv.at[c], p_s.at[c], p_r.at[c],
                      {"dp": other * group + low})

    for c in range(pieces):
        psend[c] = lax.dot_general(
            far[:, c * step:(c + 1) * step], paired[...], contract,
            preferred_element_type=jnp.float32).astype(psend.dtype)
        part_copy(c).start()

    def input_copy(to, slot):
        return remote(nxt.at[:, feature(to)], block(inputs, slot, nrows), in_s.at[to],
                      in_r.at[slot], {"dp": to})

    def other_dp(j):
        return lax.rem(me + j, n)

    each(n, lambda j: input_copy(other_dp(j), me).start())

    loads[1].wait()
    each(group, lambda j: near_copy(peer(j), peer(j)).wait_recv())
    for c in range(pieces):
        grad[c * step:(c + 1) * step, :] = lax.dot_general(
            near[:, c * step:(c + 1) * step], paired[...], contract,
            preferred_element_type=jnp.float32)

    scale = 1.0 / (tok * n)
    chunk = 32
    squares = jnp.zeros((8, cols), jnp.float32)
    for c in range(pieces):
        part_copy(c).wait_recv()

        def add(i, total):
            at = pl.multiple_of(i * chunk, chunk)
            g = (grad[pl.ds(c * step + at, chunk), :]
                 + precv[c, pl.ds(at, chunk), :].astype(jnp.float32)) * scale
            grad[pl.ds(c * step + at, chunk), :] = g
            return total + jnp.sum((g * g).reshape(chunk // 8, 8, cols), axis=0)

        squares = lax.fori_loop(0, step // chunk, add, squares)

    tile = squares[:, 0:128]
    for c in range(1, cols // 128):
        tile = tile + squares[:, c * 128:(c + 1) * 128]
    keep = jnp.where(overflow[0, 0] == 0, 1.0, 0.0)
    tile = tile * keep
    sq_mine[...] = tile

    def sq_copy(to, slot):
        return remote(sq_mine, sq_dp.at[slot], sd_s.at[to], sd_r.at[slot], {"dp": to})

    def sum_copy(to, slot):
        return remote(sq_sum, sq_sec.at[slot], ss_s.at[to], ss_r.at[slot], {"section": to})

    def other_section(j):
        return lax.rem(sec + j, sections)

    each(n, lambda j: sq_copy(other_dp(j), me).start())
    sq_dp[me] = tile
    for load in loads[2:]:
        load.wait()
    each(n, lambda j: sq_copy(other_dp(j), other_dp(j)).wait_recv())
    tile = jnp.sum(sq_dp[...], axis=0)
    sq_sum[...] = tile
    each(sections, lambda j: sum_copy(other_section(j), sec).start())
    sq_sec[sec] = tile
    each(sections, lambda j: sum_copy(other_section(j), other_section(j)).wait_recv())
    sumsq = jnp.sum(jnp.sum(sq_sec[...], axis=0), keepdims=True)
    factor = jnp.where(clip_on[0] == 1, 1.0 / jnp.maximum(jnp.sqrt(sumsq), 1.0), 1.0)
    factor = jnp.broadcast_to(factor, (1, cols))
    rate = learn_rate * keep

    def update(i, carry):
        at = pl.ds(pl.multiple_of(i * chunk, chunk), chunk)
        clipped = grad[at, :] * factor
        old = master[at, :]
        m_next = beta_one * m1[at, :] + (1.0 - beta_one) * clipped
        v_next = beta_two * m2[at, :] + (1.0 - beta_two) * (clipped * clipped)
        change = (m_next * (1.0 / correct_one)) / (
            jnp.sqrt(v_next * (1.0 / correct_two)) + adam_eps) + decay_rate * old
        new = old - rate * change
        master[at, :] = new
        weights[at, :] = new.astype(weights.dtype)
        return carry

    lax.fori_loop(0, rows // chunk, update, 0)
    store = pltpu.make_async_copy(master, master_out, load_sem.at[6])
    store.start()

    each(n, lambda j: input_copy(other_dp(j), other_dp(j)).wait_recv())
    part[...] = jnp.dot(inputs[...], weights[...], preferred_element_type=jnp.float32)

    def out_copy(to, slot):
        return remote(block(part, to, nrows), landed.at[slot], out_s.at[to], out_r.at[slot],
                      {"dp": to})

    each(n, lambda j: out_copy(other_dp(j), me).start())
    landed[me] = part[pl.ds(pl.multiple_of(me * nrows, nrows), nrows), :]
    each(n, lambda j: out_copy(other_dp(j), other_dp(j)).wait_recv())
    next_out[...] = (
        jnp.sum(landed[...], axis=0) * (1.0 / math.sqrt(width))).astype(next_out.dtype)

    each(group, lambda j: pair_copy(peer(j), low).wait_send())
    each(group, lambda j: far_copy(peer(j), low).wait_send())
    each(group, lambda j: near_copy(peer(j), low).wait_send())
    for c in range(pieces):
        part_copy(c).wait_send()
    each(n, lambda j: input_copy(other_dp(j), me).wait_send())
    each(n, lambda j: sq_copy(other_dp(j), me).wait_send())
    each(sections, lambda j: sum_copy(other_section(j), sec).wait_send())
    each(n, lambda j: out_copy(other_dp(j), me).wait_send())
    store.wait()


def local(
    activations, tail_grads, tail_slots, master, moment1, moment2, overflow, clip_on, next_inputs
):
    n = lax.axis_size("dp")
    sections = lax.axis_size("section")
    tok = activations.shape[1]
    rows, cols = master.shape[1:]
    nrows = next_inputs.shape[1]
    group = n // 2
    step = min(rows, 256)
    pieces = rows // step
    f32, bf16 = jnp.float32, jnp.bfloat16
    vmem, anywhere, smem = (
        pl.BlockSpec(memory_space=m) for m in (pltpu.VMEM, pl.ANY, pltpu.SMEM))
    dma = pltpu.SemaphoreType.DMA
    new_master, next_out = pl.pallas_call(
        functools.partial(kernel, n, sections, step),
        out_shape=(
            jax.ShapeDtypeStruct((rows, cols), f32),
            jax.ShapeDtypeStruct((nrows, cols), bf16),
        ),
        in_specs=[anywhere, vmem, smem, anywhere, anywhere, anywhere, smem, smem, anywhere],
        out_specs=(anywhere, vmem),
        scratch_shapes=[
            pltpu.VMEM((group * tok, rows), bf16),
            pltpu.VMEM((group * tok, rows), bf16),
            pltpu.VMEM((group * tok, cols), bf16),
            pltpu.VMEM((rows, cols), f32),
            pltpu.VMEM((rows, cols), f32),
            pltpu.VMEM((rows, cols), f32),
            pltpu.VMEM((rows, cols), f32),
            pltpu.VMEM((pieces, step, cols), bf16),
            pltpu.VMEM((pieces, step, cols), bf16),
            pltpu.VMEM((rows, cols), bf16),
            pltpu.VMEM((n * nrows, rows), bf16),
            pltpu.VMEM((n * nrows, cols), f32),
            pltpu.VMEM((n, nrows, cols), f32),
            pltpu.VMEM((n, 8, 128), f32),
            pltpu.VMEM((sections, 8, 128), f32),
            pltpu.VMEM((8, 128), f32),
            pltpu.VMEM((8, 128), f32),
            dma((7,)),
            dma((group,)), dma((group,)),
            dma((group,)), dma((group,)),
            dma((group,)), dma((group,)),
            dma((pieces,)), dma((pieces,)),
            dma((n,)), dma((n,)),
            dma((n,)), dma((n,)),
            dma((n,)), dma((n,)),
            dma((sections,)), dma((sections,)),
        ],
        compiler_params=pltpu.CompilerParams(
            collective_id=0, has_side_effects=True, vmem_limit_bytes=56 * 1024 * 1024),
    )(
        activations[0], tail_grads[0], tail_slots[0], master[0], moment1[0], moment2[0],
        overflow, clip_on, next_inputs[0],
    )
    return (new_master[None], next_out[None])


def solution(mesh):
    return jax.shard_map(
        local,
        mesh=mesh,
        in_specs=(
            P("section", "dp", None),
            P("section", "dp", None),
            P("section", "dp", None),
            P("section", "dp", None),
            P("section", "dp", None),
            P("section", "dp", None),
            P("section", "dp"),
            P("section"),
            P("section", "dp", None),
        ),
        out_specs=(P("section", "dp", None), P("section", "dp", None)),
        check_vma=False,
    )
```

time: 339 us -> 126 us (0.37)
  waiting for transfers between devices: 231 us -> 0 us
  Pallas kernels: 0 us -> 119 us
  blocking collectives: 37.8 us -> 0 us
  local copies, waits for them, and re-layouts: 24.3 us -> 3.7 us
  between operations: 16.8 us -> 1.94 us
  matrix products: 14 us -> 0 us
  starting transfers between devices: 7.46 us -> 0 us
  other arithmetic: 6.34 us -> 0 us
    all_gather x2 -> x0, waiting for transfers between devices: 123 us -> none  [the longest x1 123 us: local(): lax.all_gather(weights, 'dp', axis=0, tiled=True)]
    pallas_call x0 -> x1, Pallas kernels: none -> 119 us  [local(): pl.pallas_call(functools.partial(kernel, n, sections, step), out_shape=(j...]
    all_to_all x1 -> x0, waiting for transfers between devices: 108 us -> none  [local(): lax.all_to_all(stashed, 'dp', split_axis=1, concat_axis=0, tiled=True)]
    psum x1 -> x0, blocking collectives: 37.8 us -> none  [local(): sumsq = lax.psum(partial_sq, ('section', 'dp'))]
    dot_general x3 -> x0, matrix products: 14 us -> none  [the longest x1 7.12 us: local(): lax.dot_general(block, lax.all_gather(paired, 'dp', axis=0, tiled=True),...]
    unnamed x11 -> x4, local copies, waits for them, and re-layouts: 17.1 us -> 3.7 us
    all_to_all x1 -> x0, starting transfers between devices: 7.38 us -> none  [local(): lax.all_to_all(stashed, 'dp', split_axis=1, concat_axis=0, tiled=True)]
    all_to_all x1 -> x0, local copies, waits for them, and re-layouts: 6.48 us -> none  [local(): lax.all_to_all(stashed, 'dp', split_axis=1, concat_axis=0, tiled=True)]
  transfers between devices with their start and end apart: 3 -> 0, of which waited for: 2 -> 0; matrix products, arithmetic and copies ran while one was open for 5% -> 0% of each run, Pallas kernels for 0% -> 0%
where the time goes in v1:
time: 126 us; the launch traced here: 125 us
  Pallas kernels  119 us (94%)
  local copies, waits for them, and re-layouts  3.7 us (3%)
  between operations  1.94 us (2%)
    pallas_call x1, Pallas kernels, local(): pl.pallas_call(functools.partial(kernel, n, sections, step), out_shape=(j...  119 us
    unnamed x4, local copies, waits for them, and re-layouts  3.7 us

profile of v1, /device:TPU:0, one launch (start us, length us, event | category | flops | bytes accessed | tf_op | source)
XLA Modules:
  0.0 124.9 jit_solution(9914702394838900742)
XLA Ops:
  1.9 119.3 %shard_map.104 = (f32[1024,512]{1,0:T(8,128)}, bf16[32,512]{1,0:T(8,128)(2,1)}) custom-call(bf16[256,8192]{1,0:T(8,128)(2,1)} %bitcast.9, bf16[256,512]{1,0:T(8,128)(2,1)} %bitcast.15, s32[1,4]{1,0:T(1,128)} %bitcast.17, f32[1024,512]{1,0:T(8,128)} %bitcast.11, f32[1024,512]{1,0:T(8,128)} %bitcast.12, f32[1024,512]{1,0:T(8,128)} %bitcast.13, ...), custom_call_target="tpu_custom_call" | custom-call | tf_op jit(solution)/shard_map/pallas_call | solution.py:243
  121.2 0.0 copy-start
  121.2 3.1 %copy.15 = f32[1,1024,512]{2,1,0:T(8,128)} copy(f32[1,1024,512]{2,1,0:T(8,128)} %bitcast.10) | data formatting | bytes 4194304
  124.3 0.0 copy-done
  124.3 0.6 copy.16
Async XLA Ops:
  121.2 3.1 %copy-start = (bf16[32,512]{1,0:T(8,128)(2,1)S(1)}, bf16[32,512]{1,0:T(8,128)(2,1)}, u32[]{:S(2)}) copy-start(bf16[32,512]{1,0:T(8,128)(2,1)} %get-tuple-element.5) | copy-start | bytes 98308

commit v2 on v1

--- a/solution.py
+++ b/solution.py
@@ -32,7 +32,7 @@
     far, near, paired, master, m1, m2, grad, psend, precv, weights, inputs, part, landed,
     sq_dp, sq_sec, sq_mine, sq_sum,
     load_sem, far_s, far_r, near_s, near_r, pair_s, pair_r, p_s, p_r, in_s, in_r, out_s, out_r,
-    sd_s, sd_r, ss_s, ss_r,
+    sd_s, sd_r, ss_s, ss_r, relay_s,
 ):
     tok, width = act.shape
     rows, cols = master.shape
@@ -101,14 +101,33 @@
         return remote(act.at[:, feature(half * group + to)], block(near, slot, tok),
                       near_s.at[to], near_r.at[slot], {"dp": half * group + to})
 
-    each(group, lambda j: pair_copy(peer(j), low).start())
+    inner = low + 1 - 2 * lax.rem(low, 2)
+    outer = group // 2
+
+    def across(j):
+        return lax.rem(low + 2 * j, group)
+
+    def relay_copy(slot, held):
+        return remote(block(paired, held, tok), block(paired, held, tok), relay_s.at[slot],
+                      pair_r.at[held], {"dp": half * group + inner})
+
+    pair_copy(inner, low).start()
+    each(outer, lambda j: pair_copy(across(j), low).start())
     each(group, lambda j: far_copy(peer(j), low).start())
     each(group, lambda j: near_copy(peer(j), low).start())
 
+    def relay(j):
+        pair_copy(across(j), across(j)).wait_recv()
+        relay_copy(j, across(j)).start()
+
+    each(outer, relay)
+
     contract = (((0,), (0,)), ((), ()))
 
     loads[0].wait()
-    each(group, lambda j: pair_copy(peer(j), peer(j)).wait_recv())
+    pair_copy(inner, inner).wait_recv()
+    each(outer, lambda j: pair_copy(
+        inner, lax.rem(inner + 2 * j, group)).wait_recv())
     each(group, lambda j: far_copy(peer(j), peer(j)).wait_recv())
 
     def part_copy(c):
@@ -127,8 +146,6 @@
 
     def other_dp(j):
         return lax.rem(me + j, n)
-
-    each(n, lambda j: input_copy(other_dp(j), me).start())
 
     loads[1].wait()
     each(group, lambda j: near_copy(peer(j), peer(j)).wait_recv())
@@ -169,6 +186,7 @@
         return lax.rem(sec + j, sections)
 
     each(n, lambda j: sq_copy(other_dp(j), me).start())
+    each(n, lambda j: input_copy(other_dp(j), me).start())
     sq_dp[me] = tile
     for load in loads[2:]:
         load.wait()
@@ -180,40 +198,49 @@
     each(sections, lambda j: sum_copy(other_section(j), other_section(j)).wait_recv())
     sumsq = jnp.sum(jnp.sum(sq_sec[...], axis=0), keepdims=True)
     factor = jnp.where(clip_on[0] == 1, 1.0 / jnp.maximum(jnp.sqrt(sumsq), 1.0), 1.0)
-    factor = jnp.broadcast_to(factor, (1, cols))
+    side = cols // 2
+    factor = jnp.broadcast_to(factor, (1, side))
     rate = learn_rate * keep
 
-    def update(i, carry):
-        at = pl.ds(pl.multiple_of(i * chunk, chunk), chunk)
-        clipped = grad[at, :] * factor
-        old = master[at, :]
-        m_next = beta_one * m1[at, :] + (1.0 - beta_one) * clipped
-        v_next = beta_two * m2[at, :] + (1.0 - beta_two) * (clipped * clipped)
-        change = (m_next * (1.0 / correct_one)) / (
-            jnp.sqrt(v_next * (1.0 / correct_two)) + adam_eps) + decay_rate * old
-        new = old - rate * change
-        master[at, :] = new
-        weights[at, :] = new.astype(weights.dtype)
-        return carry
-
-    lax.fori_loop(0, rows // chunk, update, 0)
-    store = pltpu.make_async_copy(master, master_out, load_sem.at[6])
-    store.start()
-
-    each(n, lambda j: input_copy(other_dp(j), other_dp(j)).wait_recv())
-    part[...] = jnp.dot(inputs[...], weights[...], preferred_element_type=jnp.float32)
-
-    def out_copy(to, slot):
-        return remote(block(part, to, nrows), landed.at[slot], out_s.at[to], out_r.at[slot],
-                      {"dp": to})
-
-    each(n, lambda j: out_copy(other_dp(j), me).start())
-    landed[me] = part[pl.ds(pl.multiple_of(me * nrows, nrows), nrows), :]
-    each(n, lambda j: out_copy(other_dp(j), other_dp(j)).wait_recv())
-    next_out[...] = (
-        jnp.sum(landed[...], axis=0) * (1.0 / math.sqrt(width))).astype(next_out.dtype)
-
-    each(group, lambda j: pair_copy(peer(j), low).wait_send())
+    def out_copy(h, to, slot):
+        return remote(part.at[h, pl.ds(pl.multiple_of(to * nrows, nrows), nrows)],
+                      landed.at[h, slot], out_s.at[h, to], out_r.at[h, slot], {"dp": to})
+
+    stores = []
+    for h in range(2):
+        span = slice(h * side, (h + 1) * side)
+
+        def update(i, carry):
+            at = pl.ds(pl.multiple_of(i * chunk, chunk), chunk)
+            clipped = grad[at, span] * factor
+            old = master[at, span]
+            m_next = beta_one * m1[at, span] + (1.0 - beta_one) * clipped
+            v_next = beta_two * m2[at, span] + (1.0 - beta_two) * (clipped * clipped)
+            change = (m_next * (1.0 / correct_one)) / (
+                jnp.sqrt(v_next * (1.0 / correct_two)) + adam_eps) + decay_rate * old
+            new = old - rate * change
+            master[at, span] = new
+            weights[at, span] = new.astype(weights.dtype)
+            return carry
+
+        lax.fori_loop(0, rows // chunk, update, 0)
+        if h == 0:
+            each(n, lambda j: input_copy(other_dp(j), other_dp(j)).wait_recv())
+        part[h] = jnp.dot(inputs[...], weights[:, span], preferred_element_type=jnp.float32)
+        each(n, lambda j: out_copy(h, other_dp(j), me).start())
+        landed[h, me] = part[h, pl.ds(pl.multiple_of(me * nrows, nrows), nrows), :]
+        stores.append(pltpu.make_async_copy(
+            master.at[:, span], master_out.at[:, span], load_sem.at[6 + h]))
+        stores[h].start()
+
+    for h in range(2):
+        each(n, lambda j: out_copy(h, other_dp(j), other_dp(j)).wait_recv())
+        next_out[:, h * side:(h + 1) * side] = (
+            jnp.sum(landed[h], axis=0) * (1.0 / math.sqrt(width))).astype(next_out.dtype)
+
+    pair_copy(inner, low).wait_send()
+    each(outer, lambda j: pair_copy(across(j), low).wait_send())
+    each(outer, lambda j: relay_copy(j, across(j)).wait_send())
     each(group, lambda j: far_copy(peer(j), low).wait_send())
     each(group, lambda j: near_copy(peer(j), low).wait_send())
     for c in range(pieces):
@@ -221,8 +248,9 @@
     each(n, lambda j: input_copy(other_dp(j), me).wait_send())
     each(n, lambda j: sq_copy(other_dp(j), me).wait_send())
     each(sections, lambda j: sum_copy(other_section(j), sec).wait_send())
-    each(n, lambda j: out_copy(other_dp(j), me).wait_send())
-    store.wait()
+    for h in range(2):
+        each(n, lambda j: out_copy(h, other_dp(j), me).wait_send())
+        stores[h].wait()
 
 
 def local(
@@ -260,21 +288,22 @@
             pltpu.VMEM((pieces, step, cols), bf16),
             pltpu.VMEM((rows, cols), bf16),
             pltpu.VMEM((n * nrows, rows), bf16),
-            pltpu.VMEM((n * nrows, cols), f32),
-            pltpu.VMEM((n, nrows, cols), f32),
+            pltpu.VMEM((2, n * nrows, cols // 2), f32),
+            pltpu.VMEM((2, n, nrows, cols // 2), f32),
             pltpu.VMEM((n, 8, 128), f32),
             pltpu.VMEM((sections, 8, 128), f32),
             pltpu.VMEM((8, 128), f32),
             pltpu.VMEM((8, 128), f32),
-            dma((7,)),
+            dma((8,)),
             dma((group,)), dma((group,)),
             dma((group,)), dma((group,)),
             dma((group,)), dma((group,)),
             dma((pieces,)), dma((pieces,)),
             dma((n,)), dma((n,)),
-            dma((n,)), dma((n,)),
+            dma((2, n)), dma((2, n)),
             dma((n,)), dma((n,)),
             dma((sections,)), dma((sections,)),
+            dma((max(group // 2, 1),)),
         ],
         compiler_params=pltpu.CompilerParams(
             collective_id=0, has_side_effects=True, vmem_limit_bytes=56 * 1024 * 1024),

time: 126 us -> 142 us (1.13)
  Pallas kernels: 119 us -> 136 us
    pallas_call x1, Pallas kernels: 119 us -> 136 us  [local(): pl.pallas_call(functools.partial(kernel, n, sections, step), out_shape=(j...]
where the time goes in v2:
time: 142 us
  Pallas kernels  136 us (96%)
  local copies, waits for them, and re-layouts  3.7 us (3%)
  between operations  1.94 us (1%)
    pallas_call x1, Pallas kernels, local(): pl.pallas_call(functools.partial(kernel, n, sections, step), out_shape=(j...  136 us
    unnamed x4, local copies, waits for them, and re-layouts  3.7 us

profile of v2, /device:TPU:0, one launch (start us, length us, event | category | flops | bytes accessed | tf_op | source)
XLA Modules:
  0.0 142.0 jit_solution(3827982254335751057)
XLA Ops:
  1.9 136.3 %shard_map.104 = (f32[1024,512]{1,0:T(8,128)}, bf16[32,512]{1,0:T(8,128)(2,1)}) custom-call(bf16[256,8192]{1,0:T(8,128)(2,1)} %bitcast.9, bf16[256,512]{1,0:T(8,128)(2,1)} %bitcast.15, s32[1,4]{1,0:T(1,128)} %bitcast.17, f32[1024,512]{1,0:T(8,128)} %bitcast.11, f32[1024,512]{1,0:T(8,128)} %bitcast.12, f32[1024,512]{1,0:T(8,128)} %bitcast.13, ...), custom_call_target="tpu_custom_call" | custom-call | tf_op jit(solution)/shard_map/pallas_call | solution.py:271
  138.3 0.0 copy-start
  138.3 3.1 %copy.15 = f32[1,1024,512]{2,1,0:T(8,128)} copy(f32[1,1024,512]{2,1,0:T(8,128)} %bitcast.10) | data formatting | bytes 4194304
  141.4 0.0 copy-done
  141.4 0.6 copy.16
Async XLA Ops:
  138.3 3.1 %copy-start = (bf16[32,512]{1,0:T(8,128)(2,1)S(1)}, bf16[32,512]{1,0:T(8,128)(2,1)}, u32[]{:S(2)}) copy-start(bf16[32,512]{1,0:T(8,128)(2,1)} %get-tuple-element.5) | copy-start | bytes 98308

commit v3 on v2

--- a/solution.py
+++ b/solution.py
@@ -32,7 +32,7 @@
     far, near, paired, master, m1, m2, grad, psend, precv, weights, inputs, part, landed,
     sq_dp, sq_sec, sq_mine, sq_sum,
     load_sem, far_s, far_r, near_s, near_r, pair_s, pair_r, p_s, p_r, in_s, in_r, out_s, out_r,
-    sd_s, sd_r, ss_s, ss_r, relay_s,
+    sd_s, sd_r, ss_s, ss_r,
 ):
     tok, width = act.shape
     rows, cols = master.shape
@@ -107,27 +107,22 @@
     def across(j):
         return lax.rem(low + 2 * j, group)
 
-    def relay_copy(slot, held):
-        return remote(block(paired, held, tok), block(paired, held, tok), relay_s.at[slot],
-                      pair_r.at[held], {"dp": half * group + inner})
-
-    pair_copy(inner, low).start()
-    each(outer, lambda j: pair_copy(across(j), low).start())
-    each(group, lambda j: far_copy(peer(j), low).start())
-    each(group, lambda j: near_copy(peer(j), low).start())
-
-    def relay(j):
-        pair_copy(across(j), across(j)).wait_recv()
-        relay_copy(j, across(j)).start()
-
-    each(outer, relay)
+    each(group, lambda j: pair_copy(peer(j), low).start())
+
+    def diagonal(j):
+        return lax.rem(inner + 2 * j, group)
+
+    each(outer, lambda j: far_copy(across(j), low).start())
+    each(outer, lambda j: far_copy(diagonal(j), low).start())
+    far_copy(inner, low).start()
+    each(outer, lambda j: near_copy(across(j), low).start())
+    each(outer, lambda j: near_copy(diagonal(j), low).start())
+    near_copy(inner, low).start()
 
     contract = (((0,), (0,)), ((), ()))
 
     loads[0].wait()
-    pair_copy(inner, inner).wait_recv()
-    each(outer, lambda j: pair_copy(
-        inner, lax.rem(inner + 2 * j, group)).wait_recv())
+    each(group, lambda j: pair_copy(peer(j), peer(j)).wait_recv())
     each(group, lambda j: far_copy(peer(j), peer(j)).wait_recv())
 
     def part_copy(c):
@@ -226,7 +221,7 @@
         lax.fori_loop(0, rows // chunk, update, 0)
         if h == 0:
             each(n, lambda j: input_copy(other_dp(j), other_dp(j)).wait_recv())
-        part[h] = jnp.dot(inputs[...], weights[:, span], preferred_element_type=jnp.float32)
+        part[h] = jnp.dot(inputs[...], weights[:, span], preferred_element_type=jnp.float32).astype(part.dtype)
         each(n, lambda j: out_copy(h, other_dp(j), me).start())
         landed[h, me] = part[h, pl.ds(pl.multiple_of(me * nrows, nrows), nrows), :]
         stores.append(pltpu.make_async_copy(
@@ -236,11 +231,9 @@
     for h in range(2):
         each(n, lambda j: out_copy(h, other_dp(j), other_dp(j)).wait_recv())
         next_out[:, h * side:(h + 1) * side] = (
-            jnp.sum(landed[h], axis=0) * (1.0 / math.sqrt(width))).astype(next_out.dtype)
-
-    pair_copy(inner, low).wait_send()
-    each(outer, lambda j: pair_copy(across(j), low).wait_send())
-    each(outer, lambda j: relay_copy(j, across(j)).wait_send())
+            jnp.sum(landed[h].astype(jnp.float32), axis=0) * (1.0 / math.sqrt(width))).astype(next_out.dtype)
+
+    each(group, lambda j: pair_copy(peer(j), low).wait_send())
     each(group, lambda j: far_copy(peer(j), low).wait_send())
     each(group, lambda j: near_copy(peer(j), low).wait_send())
     for c in range(pieces):
@@ -288,8 +281,8 @@
             pltpu.VMEM((pieces, step, cols), bf16),
             pltpu.VMEM((rows, cols), bf16),
             pltpu.VMEM((n * nrows, rows), bf16),
-            pltpu.VMEM((2, n * nrows, cols // 2), f32),
-            pltpu.VMEM((2, n, nrows, cols // 2), f32),
+            pltpu.VMEM((2, n * nrows, cols // 2), bf16),
+            pltpu.VMEM((2, n, nrows, cols // 2), bf16),
             pltpu.VMEM((n, 8, 128), f32),
             pltpu.VMEM((sections, 8, 128), f32),
             pltpu.VMEM((8, 128), f32),
@@ -303,7 +296,6 @@
             dma((2, n)), dma((2, n)),
             dma((n,)), dma((n,)),
             dma((sections,)), dma((sections,)),
-            dma((max(group // 2, 1),)),
         ],
         compiler_params=pltpu.CompilerParams(
             collective_id=0, has_side_effects=True, vmem_limit_bytes=56 * 1024 * 1024),

time: 142 us -> 117 us (0.82)
  Pallas kernels: 136 us -> 112 us
    pallas_call x1, Pallas kernels: 136 us -> 112 us  [local(): pl.pallas_call(functools.partial(kernel, n, sections, step), out_shape=(j...]
where the time goes in v3:
time: 117 us
  Pallas kernels  112 us (96%)
  local copies, waits for them, and re-layouts  3.7 us (3%)
  between operations  1.94 us (2%)
    pallas_call x1, Pallas kernels, local(): pl.pallas_call(functools.partial(kernel, n, sections, step), out_shape=(j...  112 us
    unnamed x4, local copies, waits for them, and re-layouts  3.7 us

profile of v3, /device:TPU:0, one launch (start us, length us, event | category | flops | bytes accessed | tf_op | source)
XLA Modules:
  0.0 117.2 jit_solution(9448917180201781034)
XLA Ops:
  1.9 111.6 %shard_map.104 = (f32[1024,512]{1,0:T(8,128)}, bf16[32,512]{1,0:T(8,128)(2,1)}) custom-call(bf16[256,8192]{1,0:T(8,128)(2,1)} %bitcast.9, bf16[256,512]{1,0:T(8,128)(2,1)} %bitcast.15, s32[1,4]{1,0:T(1,128)} %bitcast.17, f32[1024,512]{1,0:T(8,128)} %bitcast.11, f32[1024,512]{1,0:T(8,128)} %bitcast.12, f32[1024,512]{1,0:T(8,128)} %bitcast.13, ...), custom_call_target="tpu_custom_call" | custom-call | tf_op jit(solution)/shard_map/pallas_call | solution.py:264
  113.5 0.0 copy-start
  113.5 3.1 %copy.15 = f32[1,1024,512]{2,1,0:T(8,128)} copy(f32[1,1024,512]{2,1,0:T(8,128)} %bitcast.10) | data formatting | bytes 4194304
  116.6 0.0 copy-done
  116.6 0.6 copy.16
Async XLA Ops:
  113.5 3.1 %copy-start = (bf16[32,512]{1,0:T(8,128)(2,1)S(1)}, bf16[32,512]{1,0:T(8,128)(2,1)}, u32[]{:S(2)}) copy-start(bf16[32,512]{1,0:T(8,128)(2,1)} %get-tuple-element.5) | copy-start | bytes 98308

commit v4 on v3

--- a/solution.py
+++ b/solution.py
@@ -107,7 +107,6 @@
     def across(j):
         return lax.rem(low + 2 * j, group)
 
-    each(group, lambda j: pair_copy(peer(j), low).start())
 
     def diagonal(j):
         return lax.rem(inner + 2 * j, group)
@@ -115,6 +114,7 @@
     each(outer, lambda j: far_copy(across(j), low).start())
     each(outer, lambda j: far_copy(diagonal(j), low).start())
     far_copy(inner, low).start()
+    each(group, lambda j: pair_copy(peer(j), low).start())
     each(outer, lambda j: near_copy(across(j), low).start())
     each(outer, lambda j: near_copy(diagonal(j), low).start())
     near_copy(inner, low).start()

time: 117 us -> 116 us (level)
  Pallas kernels: 112 us -> 110 us
where the time goes in v4:
time: 116 us
  Pallas kernels  110 us (95%)
  local copies, waits for them, and re-layouts  3.7 us (3%)
  between operations  1.94 us (2%)
    pallas_call x1, Pallas kernels, local(): pl.pallas_call(functools.partial(kernel, n, sections, step), out_shape=(j...  110 us
    unnamed x4, local copies, waits for them, and re-layouts  3.7 us

profile of v4, /device:TPU:0, one launch (start us, length us, event | category | flops | bytes accessed | tf_op | source)
XLA Modules:
  0.0 116.1 jit_solution(14426222171794714252)
XLA Ops:
  1.9 110.5 %shard_map.104 = (f32[1024,512]{1,0:T(8,128)}, bf16[32,512]{1,0:T(8,128)(2,1)}) custom-call(bf16[256,8192]{1,0:T(8,128)(2,1)} %bitcast.9, bf16[256,512]{1,0:T(8,128)(2,1)} %bitcast.15, s32[1,4]{1,0:T(1,128)} %bitcast.17, f32[1024,512]{1,0:T(8,128)} %bitcast.11, f32[1024,512]{1,0:T(8,128)} %bitcast.12, f32[1024,512]{1,0:T(8,128)} %bitcast.13, ...), custom_call_target="tpu_custom_call" | custom-call | tf_op jit(solution)/shard_map/pallas_call | solution.py:264
  112.4 0.0 copy-start
  112.4 3.1 %copy.15 = f32[1,1024,512]{2,1,0:T(8,128)} copy(f32[1,1024,512]{2,1,0:T(8,128)} %bitcast.10) | data formatting | bytes 4194304
  115.5 0.0 copy-done
  115.5 0.6 copy.16
Async XLA Ops:
  112.4 3.1 %copy-start = (bf16[32,512]{1,0:T(8,128)(2,1)S(1)}, bf16[32,512]{1,0:T(8,128)(2,1)}, u32[]{:S(2)}) copy-start(bf16[32,512]{1,0:T(8,128)(2,1)} %get-tuple-element.5) | copy-start | bytes 98308
